TPU v7x, 128 devices: a whole 4x4x4 slice. The times are simulated.
128 devices in a mesh: gx: 16 (over y, x), gy: 4 (over z), gz: 2 (over core).
Axes of the slice: x: 4, y: 4, z: 4, core: 2. Of those that a mesh axis runs over, the one named last changes fastest.
Arguments:
- velocity: float32 [3, 32, 256, 8192], P(None, 'gz', 'gx', 'gy'), may hold values from -6 to 6
- blade_pos: float32 [256, 3, 128], P(('gx', 'gy', 'gz')), as said below
- block_turbine: int32 [256], P(('gx', 'gy', 'gz')), may hold values from 0 to 3, as said below
- blade_vel: float32 [256, 3, 128], P(('gx', 'gy', 'gz')), may hold values from -6 to 6
- lift_coeff: float32 [256, 128], P(('gx', 'gy', 'gz')), may hold values from 0.2 to 2
Outputs:
- new_velocity: float32 [3, 32, 256, 8192], P(None, 'gz', 'gx', 'gy')
- point_force: float32 [256, 3, 128], P(('gx', 'gy', 'gz'))
Inputs may be any that keep to these rules, and one draw needn't show every extreme that they name: `block_turbine`: in each turbine row (blocks r * 4 * 2 * 2 onward, one row for each index of gx) every turbine number is named by exactly 4 blocks. `blade_pos`: the points of a block lie in its column: streamwise within its row's cells, spanwise within its turbine's cells, vertically between level 0 and the top level.
All inputs are finite; a program needn't handle non-finite values.
Results may differ from a plain program's by a relative error of at most 0.0003.
Values sent between devices are 32-bit elements; how exact they have to be, the bound alone decides.
A program may use at most 192 MiB of HBM per device.

v0:
```python
import math
import jax
import jax.numpy as jnp
from jax import lax
from jax.sharding import PartitionSpec as P

mean_wind = 1.0
viscosity = 0.2
smag_coeff = 0.17
time_step = 0.2
smear = 2.0
smear_norm = 1.0 / (smear**3 * math.pi**1.5)


def extended(cells, sides, width):
    for axis, dim in sides:
        count = lax.axis_size(axis)
        ends = count - 1
        head = lax.slice_in_dim(cells, 0, width, axis=dim)
        tail = lax.slice_in_dim(cells, cells.shape[dim] - width, cells.shape[dim], axis=dim)
        cells = jnp.concatenate(
            [
                lax.ppermute(tail, axis, [(i, (i + 1) % count) for i in range(ends)]),
                cells,
                lax.ppermute(head, axis, [((i + 1) % count, i) for i in range(ends)]),
            ],
            axis=dim,
        )
    return cells


def shifted(padded, axis_dim, offset):
    slicer = [slice(None), slice(2, -2), slice(2, -2), slice(2, -2)]
    extent = padded.shape[axis_dim] - 4
    slicer[axis_dim] = slice(2 + offset, 2 + offset + extent)
    return padded[tuple(slicer)]


def derivative(padded, axis_dim):
    near = shifted(padded, axis_dim, 1) - shifted(padded, axis_dim, -1)
    far = shifted(padded, axis_dim, 2) - shifted(padded, axis_dim, -2)
    return (8.0 * near - far) / 12.0


def second(padded, axis_dim):
    return (
        -shifted(padded, axis_dim, 2)
        + 16.0 * shifted(padded, axis_dim, 1)
        - 30.0 * shifted(padded, axis_dim, 0)
        + 16.0 * shifted(padded, axis_dim, -1)
        - shifted(padded, axis_dim, -2)
    ) / 12.0


def tendency(padded, body_force):
    along_x = derivative(padded, 2)
    along_y = derivative(padded, 3)
    along_z = derivative(padded, 1)
    gradients = (along_x, along_y, along_z)
    strain_sq = jnp.zeros(along_x.shape[1:], jnp.float32)
    for row_comp in range(3):
        for col_comp in range(3):
            strain = 0.5 * (gradients[col_comp][row_comp] + gradients[row_comp][col_comp])
            strain_sq = strain_sq + strain * strain
    eddy_visc = smag_coeff * smag_coeff * jnp.sqrt(2.0 * strain_sq)
    laplacian = second(padded, 1) + second(padded, 2) + second(padded, 3)
    return -mean_wind * along_x + (viscosity + eddy_visc[None]) * laplacian + body_force


def blade_force(sampled, blade_vel, lift_coeff):
    relative = sampled - blade_vel
    rel_speed = jnp.sqrt(jnp.sum(relative * relative, axis=1, keepdims=True))
    return -lift_coeff[:, None, :] * rel_speed * relative


def profile(anchor, count, centers):
    cells = (anchor + jnp.arange(count, dtype=jnp.int32)).astype(jnp.float32)
    gap = cells[:, None] - centers[None, :]
    return jnp.exp(-gap * gap / (smear * smear))


def local(velocity, blade_pos, block_turbine, blade_vel, lift_coeff):
    high = lax.Precision.HIGHEST
    components, depth_cells, row_cells, col_cells = velocity.shape
    owned_count = blade_pos.shape[0]
    point_count = blade_pos.shape[2]
    group_size = lax.axis_size(("gy", "gz"))
    row_blocks = owned_count * group_size
    per_turbine = row_blocks // lax.axis_size("gy")
    count = per_turbine * point_count
    turbine = lax.axis_index("gy")
    level_start = lax.axis_index("gz") * depth_cells
    row_start = lax.axis_index("gx") * row_cells
    col_start = turbine * col_cells
    padded = extended(velocity, (("gz", 1), ("gx", 2), ("gy", 3)), 2)
    row_pos, row_turb = (
        lax.all_gather(blade_pos, ("gy", "gz"), axis=0, tiled=True),
        lax.all_gather(block_turbine, ("gy", "gz"), axis=0, tiled=True),
    )
    matched = (row_turb == turbine).astype(jnp.int32)
    ranks = jnp.cumsum(matched) - 1
    slot_range = jnp.arange(per_turbine, dtype=jnp.int32)
    picker = ((ranks[None, :] == slot_range[:, None]) & (matched[None, :] == 1)).astype(jnp.float32)
    mine = jnp.einsum("ks,scp->kcp", picker, row_pos, precision=high)
    centers = mine.transpose(1, 0, 2).reshape(3, count)
    weight_x = profile(row_start, row_cells, centers[0])
    weight_y = profile(col_start, col_cells, centers[1])
    weight_z = profile(level_start, depth_cells, centers[2])
    plane = (weight_z[:, None, :] * weight_x[None, :, :]).reshape(depth_cells * row_cells, count)
    flat_vel = velocity.reshape(components * depth_cells * row_cells, col_cells)
    along = jnp.dot(flat_vel, weight_y, precision=high, preferred_element_type=jnp.float32)
    along = along.reshape(components, depth_cells * row_cells, count)
    partial_value = smear_norm * jnp.sum(along * plane[None], axis=1)
    partial_value = partial_value.reshape(components, per_turbine, point_count).transpose(1, 0, 2)
    table = jnp.einsum("ks,kcp->scp", picker, partial_value, precision=high)
    sampled = lax.psum_scatter(table, ("gy", "gz"), scatter_dimension=0, tiled=True)
    forces = blade_force(sampled, blade_vel, lift_coeff)
    row_force = lax.all_gather(forces, ("gy", "gz"), axis=0, tiled=True)
    slot_force = jnp.einsum("ks,scp->kcp", picker, row_force, precision=high)
    flat_force = slot_force.transpose(1, 0, 2).reshape(components, count)
    weighted = (smear_norm * flat_force[:, None, :] * plane[None]).reshape(
        components * depth_cells * row_cells, count
    )
    body_force = lax.dot_general(
        weighted,
        weight_y,
        (((1,), (1,)), ((), ())),
        precision=high,
        preferred_element_type=jnp.float32,
    )
    body_force = body_force.reshape(components, depth_cells, row_cells, col_cells)
    new_velocity = velocity + time_step * tendency(padded, body_force)
    return (new_velocity, forces)


def solution(mesh):
    in_specs = (
        P(None, "gz", "gx", "gy"),
        P(("gx", "gy", "gz"), None, None),
        P(("gx", "gy", "gz")),
        P(("gx", "gy", "gz"), None, None),
        P(("gx", "gy", "gz"), None),
    )
    out_specs = (P(None, "gz", "gx", "gy"), P(("gx", "gy", "gz"), None, None))
    return jax.shard_map(local, mesh=mesh, in_specs=in_specs, out_specs=out_specs, check_vma=False)
```

profile of v0, /device:TPU:24, one launch (start us, length us, event | category | flops | bytes accessed | tf_op | source)
XLA Modules:
  0.0 271.1 jit_solution(12857764865744317713)
XLA Ops:
  0.6 2.7 fusion.72
  3.3 2.6 collective-permute-start
  6.0 1.3 collective-permute-start.1
  7.3 1.4 fusion.73
  9.2 0.9 dynamic-update-slice
  10.1 12.0 %all-reduce = s32[16]{0:T(128)S(1)} all-reduce(s32[16]{0:T(128)S(1)} %dynamic-update-slice), channel_id=1, replica_groups=mesh['gx'=16,'gy'=4,'gz'=2] {'gy','gz'}, use_global_device_ids=true, to_apply=%add | all-reduce | flops 16 | bytes 128
  22.1 0.1 copy.15
  22.2 0.1 add_reduce_fusion
  22.3 0.7 copy.16
  23.0 12.8 %all_gather.10 = f32[16,3,128]{2,1,0:T(4,128)S(1)} all-gather(f32[2,3,128]{2,1,0:T(4,128)S(1)} %copy.16), channel_id=1, replica_groups=mesh['gx'=16,'gy'=4,'gz'=2] {'gy','gz'}, dimensions={0}, use_global_device_ids=true | all-gather | bytes 27648 | tf_op jit(solution)/shard_map/all_gather | solution.py:97
  35.8 0.1 convolution_bitcast_fusion
  36.0 0.0 copy-start.3
  36.0 0.0 copy-start.4
  36.0 24.0 %fusion.48 = f32[768,512]{0,1:T(8,128)S(1)} fusion(f32[768,2048]{1,0:T(8,128)} %bitcast.45, f32[512]{0:T(512)S(1)} %get-tuple-element.19, f32[2048]{0:T(1024)S(1)} %add_convert_fusion), kind=kOutput, calls=%fused_computation.67 | convolution fusion | flops 9667870720 | bytes 7874560 | tf_op jit(solution)/shard_map/dot_general | solution.py:111
  60.0 0.5 copy.18
  60.5 0.1 fusion.55
  60.6 0.1 broadcast_multiply_fusion
  60.6 0.0 copy-start.1
  60.7 0.3 multiply_reduce_fusion
  60.9 0.5 copy-done.1
  62.1 0.2 fusion.60
  62.3 23.7 %all-reduce.1 = f32[16,3,128]{2,0,1:T(8,128)S(1)} all-reduce(f32[16,3,128]{2,0,1:T(8,128)S(1)} %fusion.60), channel_id=2, replica_groups=mesh['gx'=16,'gy'=4,'gz'=2] {'gy','gz'}, use_global_device_ids=true, to_apply=%region_2.3.clone | all-reduce | flops 6144 | bytes 49152
  86.1 0.0 copy-done.3
  86.1 0.0 copy-done.4
  86.1 0.0 copy-start.2
  86.2 13.0 %all_gather.11 = f32[16,3,128]{2,1,0:T(4,128)S(1)} all-gather(f32[2,3,128]{2,1,0:T(4,128)S(1)} %copy.19), channel_id=1, replica_groups=mesh['gx'=16,'gy'=4,'gz'=2] {'gy','gz'}, dimensions={0}, use_global_device_ids=true | all-gather | bytes 27648 | tf_op jit(solution)/shard_map/all_gather | solution.py:118
  99.2 0.0 collective-permute-done
  99.2 2.5 constant_dynamic-update-slice_fusion.6
  101.6 11.8 %constant_dynamic-update-slice_fusion.4 = (f32[3,18,16,2048]{3,2,1,0:T(8,128)}, f32[3,18,16,2048]{3,2,1,0:T(8,128)}, f32[3,20,16,2048]{3,2,1,0:T(8,128)}) fusion(f32[3,16,16,2048]{3,2,1,0:T(8,128)} %param.5, f32[3,18,16,2048]{3,2,1,0:T(8,128)} %get-tuple-element.15, f32[3,20,16,2048]{3,2,1,0:T(8,128)} %get-tuple-element.16), kind=kLoop, calls=%fused_computation.89 | loop fusion | bytes 25165824
  113.5 0.0 copy-done.2
  113.5 0.0 collective-permute-done.1
  113.5 2.5 constant_dynamic-update-slice_fusion.3
  116.0 0.0 slice-start
  116.0 4.5 %fusion.71 = (f32[3,20,2,2048]{3,2,1,0:T(2,128)S(1)}, f32[3,20,2,2048]{3,2,1,0:T(2,128)S(1)}) fusion(f32[3,20,16,2048]{3,2,1,0:T(8,128)} %get-tuple-element.14), kind=kLoop, calls=%fused_computation.115 | loop fusion | bytes 3932160 | tf_op jit(solution)/shard_map/slice | solution.py:20
  120.5 4.8 %collective-permute-start.2 = (f32[3,20,2,2048]{3,2,1,0:T(2,128)S(1)}, f32[3,20,2,2048]{3,2,1,0:T(2,128)S(1)}, u32[]{:S(2)}, u32[]{:S(2)}) collective-permute-start(f32[3,20,2,2048]{3,2,1,0:T(2,128)S(1)} %get-tuple-element.7), channel_id=1, source_target_pairs={{8,0},{16,8},{24,16},{32,24},{40,32},{48,40},{56,48},{64,56},{72,6... | collective-permute-start | bytes 2949128 | tf_op jit(solution)/shard_map/ppermute | solution.py:25
  125.3 1.9 collective-permute-start.3
  127.2 0.1 fusion.51
  127.4 0.0 slice-start.1
  127.4 12.9 %subtract_multiply_fusion = f32[3,16,16,2048]{3,2,1,0:T(8,128)} fusion(f32[3,18,16,2048]{3,2,1,0:T(8,128)} %get-tuple-element.9, f32[3,18,16,2048]{3,2,1,0:T(8,128)} %get-tuple-element.13), kind=kLoop, calls=%fused_computation.18 | loop fusion | flops 7864320 | bytes 31457280 | tf_op jit(solution)/shard_map/div | solution.py:42
  140.3 6.5 %collective-permute-done.2 = f32[3,20,2,2048]{3,2,1,0:T(2,128)S(1)} collective-permute-done((f32[3,20,2,2048]{3,2,1,0:T(2,128)S(1)}, f32[3,20,2,2048]{3,2,1,0:T(2,128)S(1)}, u32[]{:S(2)}, u32[]{:S(2)}) %collective-permute-start.2) | collective-permute-done | bytes 983072 | tf_op jit(solution)/shard_map/ppermute | solution.py:25
  146.8 6.2 %collective-permute-done.3 = f32[3,20,2,2048]{3,2,1,0:T(2,128)S(1)} collective-permute-done((f32[3,20,2,2048]{3,2,1,0:T(2,128)S(1)}, f32[3,20,2,2048]{3,2,1,0:T(2,128)S(1)}, u32[]{:S(2)}, u32[]{:S(2)}) %collective-permute-start.3) | collective-permute-done | bytes 983072 | tf_op jit(solution)/shard_map/ppermute | solution.py:23
  153.0 0.0 slice-done
  153.0 0.0 slice-done.1
  153.0 0.0 copy-start
  153.0 1.3 pad_maximum_fusion.5
  154.3 1.6 copy.11
  155.9 1.3 collective-permute-start.4
  157.2 0.5 copy.13
  157.7 4.8 %collective-permute-start.5 = (f32[3,20,20,2]{2,3,1,0:T(2,128)S(1)}, f32[3,20,20,2]{2,3,1,0:T(2,128)S(1)}, u32[]{:S(2)}, u32[]{:S(2)}) collective-permute-start(f32[3,20,20,2]{2,3,1,0:T(2,128)S(1)} %copy.13), channel_id=1, source_target_pairs={{0,2},{2,4},{4,6},{1,3},{3,5},{5,7},{8,10},{10,12},{12,14},{9,11},... | collective-permute-start | bytes 28808 | tf_op jit(solution)/shard_map/ppermute | solution.py:23
  162.5 0.0 copy-done
  162.5 15.6 %fusion.7 = f32[3,16,16,2048]{3,2,1,0:T(8,128)} fusion(f32[3,20,2,2048]{3,2,1,0:T(2,128)S(1)} %collective-permute-done.2, f32[3,20,16,2048]{3,2,1,0:T(8,128)} %get-tuple-element.14, f32[3,20,2,2048]{3,2,1,0:T(2,128)S(1)} %collective-permute-done.3), kind=kLoop, calls=%fused_computation.21 | loop fusion | flops 14155776 | bytes 16121856 | tf_op jit(solution)/shard_map/div | solution.py:42
  178.1 0.0 collective-permute-done.4
  178.1 1.4 copy.12
  179.5 0.0 collective-permute-done.5
  179.5 0.0 slice-start.2
  179.5 1.4 copy.14
  180.9 0.0 slice-start.3
  180.9 21.2 %pad_maximum_fusion = (f32[3,20,20,2050]{3,2,1,0:T(8,128)}, f32[3,20,20,2050]{3,2,1,0:T(8,128)}) fusion(f32[3,20,20,2]{3,2,1,0:T(8,128)} %copy.12, f32[3,20,2,2048]{3,2,1,0:T(2,128)S(1)} %collective-permute-done.2, f32[3,20,16,2048]{3,2,1,0:T(8,128)} %get-tuple-element.14, f32[3,20,2,2048]{3,2,1,0:T(2,128)} %copy-done, f32[3,20,20,2]{3,2,1,0:T(8,128)} %copy.14), kind=kLoop, calls=%fused_computation | loop fusion | flops 14760000 | bytes 29529600 | tf_op jit(solution)/shard_map/concatenate | solution.py:21
  202.1 18.2 %subtract_multiply_fusion.1 = f32[3,16,16,2048]{3,2,1,0:T(8,128)} fusion(f32[3,20,20,2050]{3,2,1,0:T(8,128)} %get-tuple-element.3, f32[3,20,20,2050]{3,2,1,0:T(8,128)} %get-tuple-element.2), kind=kLoop, calls=%fused_computation.19 | loop fusion | flops 7864320 | bytes 31457280 | tf_op jit(solution)/shard_map/div | solution.py:42
  220.2 0.0 slice-done.2
  220.2 0.0 slice-done.3
  220.2 6.9 %fusion.23 = f32[16,16,2048]{2,1,0:T(8,128)} fusion(f32[3,16,16,2048]{3,2,1,0:T(8,128)} %subtract_multiply_fusion, f32[3,16,16,2048]{3,2,1,0:T(8,128)} %subtract_multiply_fusion.1, f32[3,16,16,2048]{3,2,1,0:T(8,128)S(1)} %bitcast.44), kind=kLoop, calls=%fused_computation.36 | loop fusion | flops 15728640 | bytes 20971520 | tf_op jit(solution)/shard_map/mul | solution.py:67
  227.1 43.8 %fusion.4 = f32[3,16,16,2048]{3,2,1,0:T(8,128)} fusion(f32[3,16,16,2048]{3,2,1,0:T(8,128)} %param.5, f32[3,20,20,2050]{3,2,1,0:T(8,128)} %get-tuple-element.3, f32[3,20,20,2050]{3,2,1,0:T(8,128)} %get-tuple-element.2, f32[3,18,16,2048]{3,2,1,0:T(8,128)} %get-tuple-element.9, f32[3,18,16,2048]{3,2,1,0:T(8,128)} %get-tuple-element.13, ...), kind=kOutput, calls=%fused_computation.13 | convolution fusion | flops 9728032768 | bytes 75382784 | tf_op jit(solution)/shard_map/dot_general | solution.py:124
  (16 shorter events, 0.1 us)
Async XLA Ops:
  3.3 95.8 %collective-permute-start = (f32[3,2,16,2048]{3,2,1,0:T(8,128)}, f32[3,2,16,2048]{3,2,1,0:T(8,128)}, u32[]{:S(2)}, u32[]{:S(2)}) collective-permute-start(f32[3,2,16,2048]{3,2,1,0:T(8,128)} %get-tuple-element.12), channel_id=1, source_target_pairs={{0,1},{2,3},{4,5},{6,7},{8,9},{10,11},{12,13},{14,15},{16,17},{18,... | collective-permute-start | bytes 2359304 | tf_op jit(solution)/shard_map/ppermute | solution.py:23
  6.0 107.5 %collective-permute-start.1 = (f32[3,2,16,2048]{3,2,1,0:T(8,128)}, f32[3,2,16,2048]{3,2,1,0:T(8,128)}, u32[]{:S(2)}, u32[]{:S(2)}) collective-permute-start(f32[3,2,16,2048]{3,2,1,0:T(8,128)} %get-tuple-element.11), channel_id=1, source_target_pairs={{1,0},{3,2},{5,4},{7,6},{9,8},{11,10},{13,12},{15,14},{17,16},{19,... | collective-permute-start | bytes 2359304 | tf_op jit(solution)/shard_map/ppermute | solution.py:25
  36.0 50.1 %copy-start.3 = (f32[2,3,128]{2,0,1:T(2,128)S(1)}, f32[2,3,128]{2,0,1:T(2,128)}, u32[]{:S(2)}) copy-start(f32[2,3,128]{2,0,1:T(2,128)} %param.8) | copy-start | bytes 9220
  36.0 50.1 %copy-start.4 = (f32[2,128]{1,0:T(2,128)S(1)}, f32[2,128]{1,0:T(2,128)}, u32[]{:S(2)}) copy-start(f32[2,128]{1,0:T(2,128)} %param.9) | copy-start | bytes 3076
  60.6 0.8 copy-start.1
  86.1 27.4 %copy-start.2 = (f32[2,3,128]{2,0,1:T(2,128)}, f32[2,3,128]{2,0,1:T(2,128)S(1)}, u32[]{:S(2)}) copy-start(f32[2,3,128]{2,0,1:T(2,128)S(1)} %broadcast_multiply_fusion.2) | copy-start | bytes 9220
  116.0 37.0 %slice-start = ((s8[7864320]{0:T(1024)(128)(4,1)}), s8[4194304]{0:T(1024)(128)(4,1)S(1)}, s32[]{:S(2)}) async-start(s8[7864320]{0:T(1024)(128)(4,1)} %bitcast.41), calls=%async_computation | async-start | bytes 8388608
  120.5 26.3 %collective-permute-start.2 = (f32[3,20,2,2048]{3,2,1,0:T(2,128)S(1)}, f32[3,20,2,2048]{3,2,1,0:T(2,128)S(1)}, u32[]{:S(2)}, u32[]{:S(2)}) collective-permute-start(f32[3,20,2,2048]{3,2,1,0:T(2,128)S(1)} %get-tuple-element.7), channel_id=1, source_target_pairs={{8,0},{16,8},{24,16},{32,24},{40,32},{48,40},{56,48},{64,56},{72,6... | collective-permute-start | bytes 2949128 | tf_op jit(solution)/shard_map/ppermute | solution.py:25
  125.3 27.7 %collective-permute-start.3 = (f32[3,20,2,2048]{3,2,1,0:T(2,128)S(1)}, f32[3,20,2,2048]{3,2,1,0:T(2,128)S(1)}, u32[]{:S(2)}, u32[]{:S(2)}) collective-permute-start(f32[3,20,2,2048]{3,2,1,0:T(2,128)S(1)} %get-tuple-element.6), channel_id=1, source_target_pairs={{0,8},{8,16},{16,24},{24,32},{32,40},{40,48},{48,56},{56,64},{64,7... | collective-permute-start | bytes 2949128 | tf_op jit(solution)/shard_map/ppermute | solution.py:23
  127.4 25.6 %slice-start.1 = ((s8[7864320]{0:T(1024)(128)(4,1)}), s8[3670016]{0:T(1024)(128)(4,1)S(1)}, s32[]{:S(2)}) async-start(s8[7864320]{0:T(1024)(128)(4,1)} %bitcast.41), calls=%async_computation.1 | async-start | bytes 7340032
  153.0 9.5 %copy-start = (f32[3,20,2,2048]{3,2,1,0:T(2,128)}, f32[3,20,2,2048]{3,2,1,0:T(2,128)S(1)}, u32[]{:S(2)}) copy-start(f32[3,20,2,2048]{3,2,1,0:T(2,128)S(1)} %collective-permute-done.3) | copy-start | bytes 2949124
  155.9 22.2 %collective-permute-start.4 = (f32[3,20,20,2]{2,3,1,0:T(2,128)S(1)}, f32[3,20,20,2]{2,3,1,0:T(2,128)S(1)}, u32[]{:S(2)}, u32[]{:S(2)}) collective-permute-start(f32[3,20,20,2]{2,3,1,0:T(2,128)S(1)} %copy.11), channel_id=1, source_target_pairs={{2,0},{4,2},{6,4},{3,1},{5,3},{7,5},{10,8},{12,10},{14,12},{11,9},... | collective-permute-start | bytes 28808 | tf_op jit(solution)/shard_map/ppermute | solution.py:25
  157.7 21.8 %collective-permute-start.5 = (f32[3,20,20,2]{2,3,1,0:T(2,128)S(1)}, f32[3,20,20,2]{2,3,1,0:T(2,128)S(1)}, u32[]{:S(2)}, u32[]{:S(2)}) collective-permute-start(f32[3,20,20,2]{2,3,1,0:T(2,128)S(1)} %copy.13), channel_id=1, source_target_pairs={{0,2},{2,4},{4,6},{1,3},{3,5},{5,7},{8,10},{10,12},{12,14},{9,11},... | collective-permute-start | bytes 28808 | tf_op jit(solution)/shard_map/ppermute | solution.py:23
  179.5 40.7 %slice-start.2 = ((s8[6291456]{0:T(1024)(128)(4,1)}), s8[2097152]{0:T(1024)(128)(4,1)S(1)}, s32[]{:S(2)}) async-start(s8[6291456]{0:T(1024)(128)(4,1)} %bitcast.43), calls=%async_computation.2 | async-start | bytes 4194304
  180.9 39.4 %slice-start.3 = ((s8[6291456]{0:T(1024)(128)(4,1)}), s8[4194304]{0:T(1024)(128)(4,1)S(1)}, s32[]{:S(2)}) async-start(s8[6291456]{0:T(1024)(128)(4,1)} %bitcast.43), calls=%async_computation.3 | async-start | bytes 8388608
where the time goes:
time: 272 us; the launch traced here: 271 us
  other arithmetic  76.7 us (28%)
  matrix products  68.2 us (25%)
  blocking collectives  61.6 us (23%)
  local copies, waits for them, and re-layouts  32.8 us (12%)
  starting transfers between devices  16.7 us (6%)
  waiting for transfers between devices  12.7 us (5%)
    div x3, other arithmetic, derivative(): return (8.0 * near - far) / 12.0  46.7 us
    dot_general x1, matrix products, local(): lax.dot_general(weighted, weight_y, (((1,), (1,)), ((), ())), precision=h...  43.8 us
    unnamed x2, blocking collectives  35.7 us
    dot_general x1, matrix products, local(): jnp.dot(flat_vel, weight_y, precision=high, preferred_element_type=jnp.fl...  24 us
    concatenate x1, other arithmetic, extended(): jnp.concatenate([lax.ppermute(tail, axis, [(i, (i + 1) % count) for i in...  21.2 us
    unnamed x25, local copies, waits for them, and re-layouts  17.8 us
    all_gather x1, blocking collectives, local(): row_force = lax.all_gather(forces, ('gy', 'gz'), axis=0, tiled=True)  13 us
    all_gather x1, blocking collectives, local(): lax.all_gather(blade_pos, ('gy', 'gz'), axis=0, tiled=True)  12.8 us
  transfers between devices with their start and end apart: 6, of which 2 were waited for; matrix products, arithmetic and copies ran while one was open for 27% of the time, Pallas kernels for 0%

commit v1 on v0

--- a/solution.py
+++ b/solution.py
@@ -115,7 +115,10 @@
     table = jnp.einsum("ks,kcp->scp", picker, partial_value, precision=high)
     sampled = lax.psum_scatter(table, ("gy", "gz"), scatter_dimension=0, tiled=True)
     forces = blade_force(sampled, blade_vel, lift_coeff)
-    row_force = lax.all_gather(forces, ("gy", "gz"), axis=0, tiled=True)
+    row_force = jnp.concatenate(
+        lax.all_to_all(jnp.stack([forces] * lax.axis_size(("gy", "gz"))), ("gy", "gz"), 0, 0),
+        axis=0,
+    )
     slot_force = jnp.einsum("ks,scp->kcp", picker, row_force, precision=high)
     flat_force = slot_force.transpose(1, 0, 2).reshape(components, count)
     weighted = (smear_norm * flat_force[:, None, :] * plane[None]).reshape(

time: 272 us -> 263 us (0.967)
  blocking collectives: 61.6 us -> 47 us
  waiting for transfers between devices: 12.7 us -> 16.1 us
  starting transfers between devices: 16.7 us -> 20 us
    all_gather x1 -> x0, blocking collectives: 13 us -> none  [local(): row_force = lax.all_gather(forces, ('gy', 'gz'), axis=0, tiled=True)]
    all_to_all x0 -> x1, waiting for transfers between devices: none -> 3.84 us  [local(): lax.all_to_all(jnp.stack([forces] * lax.axis_size(('gy', 'gz'))), ('gy',...]
    all_to_all x0 -> x1, starting transfers between devices: none -> 3.34 us  [local(): lax.all_to_all(jnp.stack([forces] * lax.axis_size(('gy', 'gz'))), ('gy',...]
  transfers between devices with their start and end apart: 6 -> 7, of which waited for: 2 -> 3; matrix products, arithmetic and copies ran while one was open for 27% -> 28% of each run, Pallas kernels for 0% -> 0%
where the time goes in v1:
time: 263 us; the launch traced here: 262 us
  other arithmetic  76.7 us (29%)
  matrix products  67.6 us (26%)
  blocking collectives  47 us (18%)
  local copies, waits for them, and re-layouts  32.3 us (12%)
  starting transfers between devices  20 us (8%)
  waiting for transfers between devices  16.1 us (6%)
    div x3, other arithmetic, derivative(): return (8.0 * near - far) / 12.0  46.7 us
    dot_general x1, matrix products, local(): lax.dot_general(weighted, weight_y, (((1,), (1,)), ((), ())), precision=h...  43.2 us
    unnamed x2, blocking collectives  34.2 us
    dot_general x1, matrix products, local(): jnp.dot(flat_vel, weight_y, precision=high, preferred_element_type=jnp.fl...  24 us
    concatenate x1, other arithmetic, extended(): jnp.concatenate([lax.ppermute(tail, axis, [(i, (i + 1) % count) for i in...  21.2 us
    unnamed x25, local copies, waits for them, and re-layouts  17.8 us
    all_gather x1, blocking collectives, local(): lax.all_gather(blade_pos, ('gy', 'gz'), axis=0, tiled=True)  12.8 us
    ppermute x3, starting transfers between devices, extended(): lax.ppermute(tail, axis, [(i, (i + 1) % count) for i in range(ends)])  9.1 us
  transfers between devices with their start and end apart: 7, of which 3 were waited for; matrix products, arithmetic and copies ran while one was open for 28% of the time, Pallas kernels for 0%

profile of v1, /device:TPU:24, one launch (start us, length us, event | category | flops | bytes accessed | tf_op | source)
XLA Modules:
  0.0 262.2 jit_solution(12501570229252102469)
XLA Ops:
  0.6 2.7 %fusion.71 = (f32[3,2,16,2048]{3,2,1,0:T(8,128)}, f32[3,2,16,2048]{3,2,1,0:T(8,128)}) fusion(f32[3,16,16,2048]{3,2,1,0:T(8,128)} %param.5), kind=kLoop, calls=%fused_computation.115 | loop fusion | bytes 3145728 | tf_op jit(solution)/shard_map/slice | solution.py:19
  3.3 2.6 %collective-permute-start = (f32[3,2,16,2048]{3,2,1,0:T(8,128)}, f32[3,2,16,2048]{3,2,1,0:T(8,128)}, u32[]{:S(2)}, u32[]{:S(2)}) collective-permute-start(f32[3,2,16,2048]{3,2,1,0:T(8,128)} %get-tuple-element.12), channel_id=1, source_target_pairs={{0,1},{2,3},{4,5},{6,7},{8,9},{10,11},{12,13},{14,15},{16,17},{18,... | collective-permute-start | bytes 2359304 | tf_op jit(solution)/shard_map/ppermute | solution.py:23
  6.0 1.4 fusion.72
  8.1 0.9 dynamic-update-slice
  8.9 10.5 %all-reduce = s32[16]{0:T(128)S(1)} all-reduce(s32[16]{0:T(128)S(1)} %dynamic-update-slice), channel_id=1, replica_groups=mesh['gx'=16,'gy'=4,'gz'=2] {'gy','gz'}, use_global_device_ids=true, to_apply=%add | all-reduce | flops 16 | bytes 128
  19.4 0.1 copy.15
  19.6 0.1 add_reduce_fusion
  19.7 0.7 copy.16
  20.4 12.8 %all_gather.7 = f32[16,3,128]{2,1,0:T(4,128)S(1)} all-gather(f32[2,3,128]{2,1,0:T(4,128)S(1)} %copy.16), channel_id=1, replica_groups=mesh['gx'=16,'gy'=4,'gz'=2] {'gy','gz'}, dimensions={0}, use_global_device_ids=true | all-gather | bytes 27648 | tf_op jit(solution)/shard_map/all_gather | solution.py:97
  33.2 0.1 convolution_bitcast_fusion
  33.3 0.0 copy-start.3
  33.4 0.0 copy-start.4
  33.4 24.0 %fusion.48 = f32[768,512]{0,1:T(8,128)S(1)} fusion(f32[768,2048]{1,0:T(8,128)} %bitcast.47, f32[512]{0:T(512)S(1)} %get-tuple-element.19, f32[2048]{0:T(1024)S(1)} %add_convert_fusion), kind=kOutput, calls=%fused_computation.67 | convolution fusion | flops 9667870720 | bytes 7874560 | tf_op jit(solution)/shard_map/dot_general | solution.py:111
  57.3 0.5 copy.18
  57.8 0.1 fusion.55
  57.9 0.1 broadcast_multiply_fusion
  58.0 0.0 copy-start.1
  58.0 0.3 multiply_reduce_fusion
  58.2 0.5 copy-done.1
  59.5 0.2 fusion.59
  59.7 23.7 %all-reduce.1 = f32[16,3,128]{2,0,1:T(8,128)S(1)} all-reduce(f32[16,3,128]{2,0,1:T(8,128)S(1)} %fusion.59), channel_id=2, replica_groups=mesh['gx'=16,'gy'=4,'gz'=2] {'gy','gz'}, use_global_device_ids=true, to_apply=%region_2.3.clone | all-reduce | flops 6144 | bytes 49152
  83.4 0.0 copy-done.3
  83.4 0.0 copy-done.4
  83.5 0.0 copy-start.2
  83.5 0.6 stack.2
  84.1 3.3 %all-to-all-start = ((f32[8,2,3,128]{3,1,2,0:T(2,128)}), f32[8,2,3,128]{3,1,2,0:T(2,128)S(1)}, u32[]{:S(2)}, u32[]{:S(2)}) async-start(f32[8,2,3,128]{3,1,2,0:T(2,128)} %stack.2), calls=%async_computation | async-start | bytes 49152 | tf_op jit(solution)/shard_map/all_to_all | solution.py:119
  87.4 1.5 collective-permute-start.1
  88.9 3.8 %all-to-all-done = f32[8,2,3,128]{3,1,2,0:T(2,128)S(1)} async-done(((f32[8,2,3,128]{3,1,2,0:T(2,128)}), f32[8,2,3,128]{3,1,2,0:T(2,128)S(1)}, u32[]{:S(2)}, u32[]{:S(2)}) %all-to-all-start) | async-done | bytes 24608 | tf_op jit(solution)/shard_map/all_to_all | solution.py:119
  92.8 0.0 collective-permute-done
  92.8 2.5 constant_dynamic-update-slice_fusion.6
  95.2 11.8 %constant_dynamic-update-slice_fusion.4 = (f32[3,18,16,2048]{3,2,1,0:T(8,128)}, f32[3,18,16,2048]{3,2,1,0:T(8,128)}, f32[3,20,16,2048]{3,2,1,0:T(8,128)}) fusion(f32[3,16,16,2048]{3,2,1,0:T(8,128)} %param.5, f32[3,18,16,2048]{3,2,1,0:T(8,128)} %get-tuple-element.15, f32[3,20,16,2048]{3,2,1,0:T(8,128)} %get-tuple-element.16), kind=kLoop, calls=%fused_computation.88 | loop fusion | bytes 25165824
  107.0 0.0 copy-done.2
  107.0 0.0 collective-permute-done.1
  107.1 1.4 constant_dynamic-update-slice_fusion.3
  108.4 0.0 slice-start
  108.4 4.5 %fusion.70 = (f32[3,20,2,2048]{3,2,1,0:T(2,128)S(1)}, f32[3,20,2,2048]{3,2,1,0:T(2,128)S(1)}) fusion(f32[3,20,16,2048]{3,2,1,0:T(8,128)} %get-tuple-element.14), kind=kLoop, calls=%fused_computation.114 | loop fusion | bytes 3932160 | tf_op jit(solution)/shard_map/slice | solution.py:20
  112.9 4.8 %collective-permute-start.2 = (f32[3,20,2,2048]{3,2,1,0:T(2,128)S(1)}, f32[3,20,2,2048]{3,2,1,0:T(2,128)S(1)}, u32[]{:S(2)}, u32[]{:S(2)}) collective-permute-start(f32[3,20,2,2048]{3,2,1,0:T(2,128)S(1)} %get-tuple-element.7), channel_id=1, source_target_pairs={{8,0},{16,8},{24,16},{32,24},{40,32},{48,40},{56,48},{64,56},{72,6... | collective-permute-start | bytes 2949128 | tf_op jit(solution)/shard_map/ppermute | solution.py:25
  117.8 1.9 collective-permute-start.3
  119.7 0.1 fusion.51
  119.8 0.0 slice-start.1
  119.8 12.9 %subtract_multiply_fusion = f32[3,16,16,2048]{3,2,1,0:T(8,128)} fusion(f32[3,18,16,2048]{3,2,1,0:T(8,128)} %get-tuple-element.9, f32[3,18,16,2048]{3,2,1,0:T(8,128)} %get-tuple-element.13), kind=kLoop, calls=%fused_computation.18 | loop fusion | flops 7864320 | bytes 31457280 | tf_op jit(solution)/shard_map/div | solution.py:42
  132.7 6.0 %collective-permute-done.2 = f32[3,20,2,2048]{3,2,1,0:T(2,128)S(1)} collective-permute-done((f32[3,20,2,2048]{3,2,1,0:T(2,128)S(1)}, f32[3,20,2,2048]{3,2,1,0:T(2,128)S(1)}, u32[]{:S(2)}, u32[]{:S(2)}) %collective-permute-start.2) | collective-permute-done | bytes 983072 | tf_op jit(solution)/shard_map/ppermute | solution.py:25
  138.7 6.2 %collective-permute-done.3 = f32[3,20,2,2048]{3,2,1,0:T(2,128)S(1)} collective-permute-done((f32[3,20,2,2048]{3,2,1,0:T(2,128)S(1)}, f32[3,20,2,2048]{3,2,1,0:T(2,128)S(1)}, u32[]{:S(2)}, u32[]{:S(2)}) %collective-permute-start.3) | collective-permute-done | bytes 983072 | tf_op jit(solution)/shard_map/ppermute | solution.py:23
  144.9 0.0 slice-done
  144.9 0.0 slice-done.1
  144.9 0.0 copy-start
  144.9 1.4 pad_maximum_fusion.5
  146.3 1.6 copy.11
  147.9 1.3 collective-permute-start.4
  149.2 0.5 copy.13
  149.6 4.5 %collective-permute-start.5 = (f32[3,20,20,2]{2,3,1,0:T(2,128)S(1)}, f32[3,20,20,2]{2,3,1,0:T(2,128)S(1)}, u32[]{:S(2)}, u32[]{:S(2)}) collective-permute-start(f32[3,20,20,2]{2,3,1,0:T(2,128)S(1)} %copy.13), channel_id=1, source_target_pairs={{0,2},{2,4},{4,6},{1,3},{3,5},{5,7},{8,10},{10,12},{12,14},{9,11},... | collective-permute-start | bytes 28808 | tf_op jit(solution)/shard_map/ppermute | solution.py:23
  154.2 0.0 copy-done
  154.2 15.6 %fusion.7 = f32[3,16,16,2048]{3,2,1,0:T(8,128)} fusion(f32[3,20,2,2048]{3,2,1,0:T(2,128)S(1)} %collective-permute-done.2, f32[3,20,16,2048]{3,2,1,0:T(8,128)} %get-tuple-element.14, f32[3,20,2,2048]{3,2,1,0:T(2,128)S(1)} %collective-permute-done.3), kind=kLoop, calls=%fused_computation.21 | loop fusion | flops 14155776 | bytes 16121856 | tf_op jit(solution)/shard_map/div | solution.py:42
  169.8 0.0 collective-permute-done.4
  169.8 1.4 copy.12
  171.2 0.0 collective-permute-done.5
  171.2 0.0 slice-start.2
  171.2 1.3 copy.14
  172.6 21.2 %pad_maximum_fusion = (f32[3,20,20,2050]{3,2,1,0:T(8,128)}, f32[3,20,20,2050]{3,2,1,0:T(8,128)}) fusion(f32[3,20,20,2]{3,2,1,0:T(8,128)} %copy.12, f32[3,20,2,2048]{3,2,1,0:T(2,128)S(1)} %collective-permute-done.2, f32[3,20,16,2048]{3,2,1,0:T(8,128)} %get-tuple-element.14, f32[3,20,2,2048]{3,2,1,0:T(2,128)} %copy-done, f32[3,20,20,2]{3,2,1,0:T(8,128)} %copy.14), kind=kLoop, calls=%fused_computation | loop fusion | flops 14760000 | bytes 29529600 | tf_op jit(solution)/shard_map/concatenate | solution.py:21
  193.7 18.2 %subtract_multiply_fusion.1 = f32[3,16,16,2048]{3,2,1,0:T(8,128)} fusion(f32[3,20,20,2050]{3,2,1,0:T(8,128)} %get-tuple-element.3, f32[3,20,20,2050]{3,2,1,0:T(8,128)} %get-tuple-element.2), kind=kLoop, calls=%fused_computation.19 | loop fusion | flops 7864320 | bytes 31457280 | tf_op jit(solution)/shard_map/div | solution.py:42
  211.9 0.0 slice-done.2
  211.9 0.0 slice-done.3
  211.9 6.9 %fusion.23 = f32[16,16,2048]{2,1,0:T(8,128)} fusion(f32[3,16,16,2048]{3,2,1,0:T(8,128)} %subtract_multiply_fusion, f32[3,16,16,2048]{3,2,1,0:T(8,128)} %subtract_multiply_fusion.1, f32[3,16,16,2048]{3,2,1,0:T(8,128)S(1)} %bitcast.46), kind=kLoop, calls=%fused_computation.36 | loop fusion | flops 15728640 | bytes 20971520 | tf_op jit(solution)/shard_map/mul | solution.py:67
  218.8 43.2 %fusion.4 = f32[3,16,16,2048]{3,2,1,0:T(8,128)} fusion(f32[3,16,16,2048]{3,2,1,0:T(8,128)} %param.5, f32[3,20,20,2050]{3,2,1,0:T(8,128)} %get-tuple-element.3, f32[3,20,20,2050]{3,2,1,0:T(8,128)} %get-tuple-element.2, f32[3,18,16,2048]{3,2,1,0:T(8,128)} %get-tuple-element.9, f32[3,18,16,2048]{3,2,1,0:T(8,128)} %get-tuple-element.13, ...), kind=kOutput, calls=%fused_computation.13 | convolution fusion | flops 9728032768 | bytes 75382784 | tf_op jit(solution)/shard_map/dot_general | solution.py:127
  (17 shorter events, 0.1 us)
Async XLA Ops:
  3.3 89.4 %collective-permute-start = (f32[3,2,16,2048]{3,2,1,0:T(8,128)}, f32[3,2,16,2048]{3,2,1,0:T(8,128)}, u32[]{:S(2)}, u32[]{:S(2)}) collective-permute-start(f32[3,2,16,2048]{3,2,1,0:T(8,128)} %get-tuple-element.12), channel_id=1, source_target_pairs={{0,1},{2,3},{4,5},{6,7},{8,9},{10,11},{12,13},{14,15},{16,17},{18,... | collective-permute-start | bytes 2359304 | tf_op jit(solution)/shard_map/ppermute | solution.py:23
  33.3 50.0 %copy-start.3 = (f32[2,3,128]{2,0,1:T(2,128)S(1)}, f32[2,3,128]{2,0,1:T(2,128)}, u32[]{:S(2)}) copy-start(f32[2,3,128]{2,0,1:T(2,128)} %param.8) | copy-start | bytes 9220
  33.4 50.1 %copy-start.4 = (f32[2,128]{1,0:T(2,128)S(1)}, f32[2,128]{1,0:T(2,128)}, u32[]{:S(2)}) copy-start(f32[2,128]{1,0:T(2,128)} %param.9) | copy-start | bytes 3076
  58.0 0.8 copy-start.1
  83.5 23.6 %copy-start.2 = (f32[2,3,128]{2,0,1:T(2,128)}, f32[2,3,128]{2,0,1:T(2,128)S(1)}, u32[]{:S(2)}) copy-start(f32[2,3,128]{2,0,1:T(2,128)S(1)} %broadcast_multiply_fusion.2) | copy-start | bytes 9220
  84.1 8.7 %all-to-all-start = ((f32[8,2,3,128]{3,1,2,0:T(2,128)}), f32[8,2,3,128]{3,1,2,0:T(2,128)S(1)}, u32[]{:S(2)}, u32[]{:S(2)}) async-start(f32[8,2,3,128]{3,1,2,0:T(2,128)} %stack.2), calls=%async_computation | async-start | bytes 49152 | tf_op jit(solution)/shard_map/all_to_all | solution.py:119
  87.4 19.6 %collective-permute-start.1 = (f32[3,2,16,2048]{3,2,1,0:T(8,128)}, f32[3,2,16,2048]{3,2,1,0:T(8,128)S(1)}, u32[]{:S(2)}, u32[]{:S(2)}) collective-permute-start(f32[3,2,16,2048]{3,2,1,0:T(8,128)} %get-tuple-element.11), channel_id=1, source_target_pairs={{1,0},{3,2},{5,4},{7,6},{9,8},{11,10},{13,12},{15,14},{17,16},{19,... | collective-permute-start | bytes 2359304 | tf_op jit(solution)/shard_map/ppermute | solution.py:25
  108.4 36.5 %slice-start = ((s8[7864320]{0:T(1024)(128)(4,1)}), s8[4194304]{0:T(1024)(128)(4,1)S(1)}, s32[]{:S(2)}) async-start(s8[7864320]{0:T(1024)(128)(4,1)} %bitcast.43), calls=%async_computation.1 | async-start | bytes 8388608
  112.9 25.8 %collective-permute-start.2 = (f32[3,20,2,2048]{3,2,1,0:T(2,128)S(1)}, f32[3,20,2,2048]{3,2,1,0:T(2,128)S(1)}, u32[]{:S(2)}, u32[]{:S(2)}) collective-permute-start(f32[3,20,2,2048]{3,2,1,0:T(2,128)S(1)} %get-tuple-element.7), channel_id=1, source_target_pairs={{8,0},{16,8},{24,16},{32,24},{40,32},{48,40},{56,48},{64,56},{72,6... | collective-permute-start | bytes 2949128 | tf_op jit(solution)/shard_map/ppermute | solution.py:25
  117.8 27.2 %collective-permute-start.3 = (f32[3,20,2,2048]{3,2,1,0:T(2,128)S(1)}, f32[3,20,2,2048]{3,2,1,0:T(2,128)S(1)}, u32[]{:S(2)}, u32[]{:S(2)}) collective-permute-start(f32[3,20,2,2048]{3,2,1,0:T(2,128)S(1)} %get-tuple-element.6), channel_id=1, source_target_pairs={{0,8},{8,16},{16,24},{24,32},{32,40},{40,48},{48,56},{56,64},{64,7... | collective-permute-start | bytes 2949128 | tf_op jit(solution)/shard_map/ppermute | solution.py:23
  119.8 25.1 %slice-start.1 = ((s8[7864320]{0:T(1024)(128)(4,1)}), s8[3670016]{0:T(1024)(128)(4,1)S(1)}, s32[]{:S(2)}) async-start(s8[7864320]{0:T(1024)(128)(4,1)} %bitcast.43), calls=%async_computation.2 | async-start | bytes 7340032
  144.9 9.3 %copy-start = (f32[3,20,2,2048]{3,2,1,0:T(2,128)}, f32[3,20,2,2048]{3,2,1,0:T(2,128)S(1)}, u32[]{:S(2)}) copy-start(f32[3,20,2,2048]{3,2,1,0:T(2,128)S(1)} %collective-permute-done.3) | copy-start | bytes 2949124
  147.9 22.0 %collective-permute-start.4 = (f32[3,20,20,2]{2,3,1,0:T(2,128)S(1)}, f32[3,20,20,2]{2,3,1,0:T(2,128)S(1)}, u32[]{:S(2)}, u32[]{:S(2)}) collective-permute-start(f32[3,20,20,2]{2,3,1,0:T(2,128)S(1)} %copy.11), channel_id=1, source_target_pairs={{2,0},{4,2},{6,4},{3,1},{5,3},{7,5},{10,8},{12,10},{14,12},{11,9},... | collective-permute-start | bytes 28808 | tf_op jit(solution)/shard_map/ppermute | solution.py:25
  149.6 21.6 %collective-permute-start.5 = (f32[3,20,20,2]{2,3,1,0:T(2,128)S(1)}, f32[3,20,20,2]{2,3,1,0:T(2,128)S(1)}, u32[]{:S(2)}, u32[]{:S(2)}) collective-permute-start(f32[3,20,20,2]{2,3,1,0:T(2,128)S(1)} %copy.13), channel_id=1, source_target_pairs={{0,2},{2,4},{4,6},{1,3},{3,5},{5,7},{8,10},{10,12},{12,14},{9,11},... | collective-permute-start | bytes 28808 | tf_op jit(solution)/shard_map/ppermute | solution.py:23
  171.2 40.7 %slice-start.2 = ((s8[6291456]{0:T(1024)(128)(4,1)}), s8[2097152]{0:T(1024)(128)(4,1)S(1)}, s32[]{:S(2)}) async-start(s8[6291456]{0:T(1024)(128)(4,1)} %bitcast.45), calls=%async_computation.3 | async-start | bytes 4194304
  172.6 39.3 %slice-start.3 = ((s8[6291456]{0:T(1024)(128)(4,1)}), s8[4194304]{0:T(1024)(128)(4,1)S(1)}, s32[]{:S(2)}) async-start(s8[6291456]{0:T(1024)(128)(4,1)} %bitcast.45), calls=%async_computation.4 | async-start | bytes 8388608
